TPU v7x, 32 devices: a whole 2x2x4 slice. The times are simulated.
32 devices in a mesh: groups: 2 (over y), graph: 4 (over z), pipe: 2 (over x), feat: 2 (over core).
Axes of the slice: x: 2, y: 2, z: 4, core: 2. Of those that a mesh axis runs over, the one named last changes fastest.
Arguments:
- atom_state: bfloat16 [4, 32, 512], P(('groups', 'pipe'), 'graph'), parts along dimension 0, may hold values from -6 to 6
- direction: bfloat16 [4, 32, 512], P(('groups', 'pipe'), 'graph'), parts along dimension 0, may hold values from -6 to 6
- upstream: bfloat16 [4, 32, 512], P(('groups', 'pipe'), 'graph'), parts along dimension 0, may hold values from -6 to 6
- edge_state: bfloat16 [4, 2048, 512], P(('groups', 'pipe'), 'graph'), parts along dimension 0, may hold values from -6 to 6
- edge_src: int32 [4, 2048], P(('groups', 'pipe'), 'graph'), parts along dimension 0, may hold values from 0 to 31
- edge_tgt: int32 [4, 2048], P(('groups', 'pipe'), 'graph'), parts along dimension 0, may hold values from 0 to 31
- edge_blocks: int32 [4, 4], P(('groups', 'pipe'), 'graph'), parts along dimension 0, may hold values from 1 to 4, as said below
- trip_in: int32 [4, 1024], P(('groups', 'pipe'), 'graph'), parts along dimension 0, may hold values from 0 to 511, as said below
- trip_out: int32 [4, 1024], P(('groups', 'pipe'), 'graph'), parts along dimension 0, may hold values from 0 to 511, as said below
- trip_coef: bfloat16 [4, 1024], P(('groups', 'pipe'), 'graph'), parts along dimension 0, may hold values from -1 to 1
- w_src: bfloat16 [512, 512], replicated, may hold values from -0.25 to 0.25
- w_tgt: bfloat16 [512, 512], replicated, may hold values from -0.25 to 0.25
- w_in: bfloat16 [512, 1024], P(None, 'feat'), may hold values from -0.25 to 0.25
- w_out: bfloat16 [1024, 512], P('feat'), may hold values from -0.03125 to 0.03125
Outputs:
- atom_update: bfloat16 [4, 32, 512], P(('groups', 'pipe'), 'graph'), parts along dimension 0
- grad_state: float32 [4, 32, 512], P(('groups', 'pipe'), 'graph'), parts along dimension 0
- hvp_state: float32 [4, 32, 512], P(('groups', 'pipe'), 'graph'), parts along dimension 0
There are 2 independent parts, one for each index of `groups`. A program takes and returns all parts, laid end to end along the dimension named above; an argument that names none is the same for every part. Nothing has to cross between parts.
Inputs may be any that keep to these rules, and one draw needn't show every extreme that they name: `edge_blocks`: number of leading blocks of 128 edge slots of one device that hold edges; the other slots of that device are padding, whatever ids they carry. In every micro-batch some device is full. `trip_in`: A slot of the same device that holds an edge. `trip_out`: A slot of the same device that holds an edge.
All inputs are finite; a program needn't handle non-finite values.
Results may differ from a plain program's by a relative error of at most 0.0049.
Values may be sent and summed in bfloat16 or wider, within the bound.
A program may use at most 64 MiB of HBM per device.

v0:
```python
import jax
import jax.numpy as jnp
from jax import lax
from jax.sharding import PartitionSpec as P

EBLOCK = 128


def hot_rows(slot_ids, row_count):
    columns = lax.broadcasted_iota(jnp.int32, (slot_ids.shape[0], row_count), 1)
    return (slot_ids[:, None] == columns).astype(jnp.bfloat16)


def slot_block(values, ordinal):
    return lax.dynamic_slice_in_dim(values, ordinal * EBLOCK, EBLOCK, 0)


def select_rows(totals, src_rows, tgt_rows, src_ids, tgt_ids, valid_blocks):
    row_count = src_rows.shape[0]

    def select_one_block(ordinal, running):
        src_part = jnp.dot(
            hot_rows(slot_block(src_ids, ordinal), row_count),
            src_rows,
            preferred_element_type=jnp.float32,
        )
        tgt_part = jnp.dot(
            hot_rows(slot_block(tgt_ids, ordinal), row_count),
            tgt_rows,
            preferred_element_type=jnp.float32,
        )
        first_row = ordinal * EBLOCK
        src_total = lax.dynamic_update_slice_in_dim(
            running[0], slot_block(running[0], ordinal) + src_part, first_row, 0
        )
        tgt_total = lax.dynamic_update_slice_in_dim(
            running[1], slot_block(running[1], ordinal) + tgt_part, first_row, 0
        )
        return (src_total, tgt_total)

    return lax.fori_loop(0, valid_blocks, select_one_block, totals)


def project_cols(values, weight_cols):
    return jnp.einsum(
        "ac,kc->ak",
        values,
        weight_cols.astype(jnp.float32),
        precision=lax.Precision.HIGHEST,
        preferred_element_type=jnp.float32,
    )


def on_device(
    atom_state,
    direction,
    upstream,
    edge_state,
    edge_src,
    edge_tgt,
    edge_blocks,
    trip_in,
    trip_out,
    trip_coef,
    w_src,
    w_tgt,
    w_in,
    w_out,
):
    emb_width = atom_state.shape[2]
    atom_count = atom_state.shape[1]
    slot_count = edge_state.shape[1]
    valid_blocks = edge_blocks[0, 0]
    src_ids = edge_src[0]
    tgt_ids = edge_tgt[0]
    empty_rows = (
        jnp.zeros((slot_count, 2 * emb_width), jnp.float32),
        jnp.zeros((slot_count, 3 * emb_width), jnp.float32),
    )
    w_both = jnp.concatenate([w_src, w_tgt], axis=1)
    state_proj = jnp.dot(atom_state[0], w_both, preferred_element_type=jnp.float32).astype(
        jnp.bfloat16
    )
    tan_proj = jnp.dot(direction[0], w_both, preferred_element_type=jnp.float32).astype(
        jnp.bfloat16
    )
    src_rows = jnp.concatenate([state_proj[:, :emb_width], tan_proj[:, :emb_width]], axis=1)
    tgt_rows = jnp.concatenate(
        [state_proj[:, emb_width:], tan_proj[:, emb_width:], upstream[0]], axis=1
    )
    sel_src, sel_tgt = select_rows(
        empty_rows,
        lax.all_gather(src_rows, "graph", axis=0, tiled=True),
        lax.all_gather(tgt_rows, "graph", axis=0, tiled=True),
        src_ids,
        tgt_ids,
        valid_blocks,
    )
    slot_iota = lax.broadcasted_iota(jnp.int32, (slot_count, 1), 0)
    slot_mask = (slot_iota < valid_blocks * EBLOCK).astype(jnp.float32)
    pre_edge = edge_state[0].astype(jnp.float32) + sel_src[:, :emb_width] + sel_tgt[:, :emb_width]
    tan_edge = sel_src[:, emb_width:] + sel_tgt[:, emb_width : 2 * emb_width]
    edge_cot = (slot_mask * sel_tgt[:, 2 * emb_width :]).astype(jnp.bfloat16)
    edge_pair = jnp.concatenate([pre_edge, tan_edge], axis=1)
    slot_columns = lax.broadcasted_iota(jnp.int32, (trip_in.shape[1], slot_count), 1)
    in_hot = (trip_in[0][:, None] == slot_columns).astype(jnp.bfloat16)
    out_hot = (trip_out[0][:, None] == slot_columns).astype(jnp.bfloat16)
    coef_col = trip_coef[0][:, None]
    in_weighted = in_hot * coef_col
    out_weighted = out_hot * coef_col
    picked = jnp.dot(
        in_hot, edge_pair.astype(jnp.bfloat16), preferred_element_type=jnp.float32
    ).astype(jnp.bfloat16)
    own_rows = slot_count // lax.axis_size("feat")
    own_start = lax.axis_index("feat") * own_rows
    weight_in, weight_out = (
        lax.all_gather(w_in, "feat", axis=1, tiled=True),
        lax.all_gather(w_out, "feat", axis=0, tiled=True),
    )
    own_weighted = lax.dynamic_slice_in_dim(out_weighted, own_start, own_rows, 1)
    own_mask = lax.dynamic_slice_in_dim(slot_mask, own_start, own_rows, 0)
    own_cot = lax.dynamic_slice_in_dim(edge_cot, own_start, own_rows, 0)
    own_pair = lax.dynamic_slice_in_dim(edge_pair, own_start, own_rows, 0)
    mixed_sum = own_pair + jnp.einsum(
        "te,tc->ec", own_weighted, picked, preferred_element_type=jnp.float32
    )
    mixed_low = mixed_sum.astype(jnp.bfloat16)
    hidden_pre = jnp.dot(mixed_low[:, :emb_width], weight_in, preferred_element_type=jnp.float32)
    tan_hidden = jnp.dot(mixed_low[:, emb_width:], weight_in, preferred_element_type=jnp.float32)
    sig_hidden = jax.nn.sigmoid(hidden_pre)
    activation = (hidden_pre * sig_hidden).astype(jnp.bfloat16)
    message = own_mask * jnp.dot(activation, weight_out, preferred_element_type=jnp.float32)
    act_cot = jnp.einsum("ed,hd->eh", own_cot, weight_out, preferred_element_type=jnp.float32)
    first_slope = sig_hidden * (1.0 + hidden_pre * (1.0 - sig_hidden))
    second_slope = sig_hidden * (1.0 - sig_hidden) * (2.0 + hidden_pre * (1.0 - 2.0 * sig_hidden))
    hid_cot = (act_cot * first_slope).astype(jnp.bfloat16)
    tan_hid_cot = (act_cot * second_slope * tan_hidden).astype(jnp.bfloat16)
    part_cot = jnp.einsum("eh,dh->ed", hid_cot, weight_in, preferred_element_type=jnp.float32)
    part_tan = jnp.einsum("eh,dh->ed", tan_hid_cot, weight_in, preferred_element_type=jnp.float32)
    cot_pair = lax.all_gather(
        jnp.concatenate([part_cot, part_tan], axis=1), "feat", axis=0, tiled=True
    )
    keep_mask = ((slot_iota >= own_start) & (slot_iota < own_start + own_rows)).astype(jnp.bfloat16)
    message = lax.dynamic_update_slice_in_dim(
        jnp.zeros((slot_count, emb_width), jnp.float32), message, own_start, 0
    )
    back_picked = jnp.dot(
        out_hot, cot_pair.astype(jnp.bfloat16), preferred_element_type=jnp.float32
    ).astype(jnp.bfloat16)
    pre_cot = cot_pair + jnp.einsum(
        "te,tc->ec", in_weighted, back_picked, preferred_element_type=jnp.float32
    )
    pre_cot_low = pre_cot.astype(jnp.bfloat16) * keep_mask

    def atom_one_block(ordinal, running):
        src_hot = hot_rows(slot_block(src_ids, ordinal), lax.axis_size("graph") * atom_count)
        tgt_hot = hot_rows(slot_block(tgt_ids, ordinal), lax.axis_size("graph") * atom_count)
        update_part = jnp.einsum(
            "ea,ed->ad",
            tgt_hot.astype(jnp.float32),
            slot_block(message, ordinal),
            precision=lax.Precision.HIGHEST,
            preferred_element_type=jnp.float32,
        )
        cot_rows = slot_block(pre_cot_low, ordinal)
        via_src = jnp.einsum("ea,ec->ac", src_hot, cot_rows, preferred_element_type=jnp.float32)
        via_tgt = jnp.einsum("ea,ec->ac", tgt_hot, cot_rows, preferred_element_type=jnp.float32)
        return running + jnp.concatenate([update_part, via_src, via_tgt], axis=1)

    summed = lax.psum_scatter(
        lax.fori_loop(
            0,
            valid_blocks,
            atom_one_block,
            jnp.zeros(
                (lax.axis_size("graph") * atom_count, emb_width + 4 * emb_width), jnp.float32
            ),
        ),
        "graph",
        scatter_dimension=0,
        tiled=True,
    )
    update_part = summed[:, :emb_width]
    via_src = summed[:, emb_width : emb_width + 2 * emb_width]
    via_tgt = summed[:, emb_width + 2 * emb_width :]
    grad_part = project_cols(via_src[:, :emb_width], w_src) + project_cols(
        via_tgt[:, :emb_width], w_tgt
    )
    hvp_part = project_cols(via_src[:, emb_width:], w_src) + project_cols(
        via_tgt[:, emb_width:], w_tgt
    )
    update_sum, grad_state, hvp_state = lax.psum((update_part, grad_part, hvp_part), "feat")
    return (update_sum.astype(jnp.bfloat16)[None], grad_state[None], hvp_state[None])


def solution(mesh):
    in_specs = (
        P(("groups", "pipe"), "graph", None),
        P(("groups", "pipe"), "graph", None),
        P(("groups", "pipe"), "graph", None),
        P(("groups", "pipe"), "graph", None),
        P(("groups", "pipe"), "graph"),
        P(("groups", "pipe"), "graph"),
        P(("groups", "pipe"), "graph"),
        P(("groups", "pipe"), "graph"),
        P(("groups", "pipe"), "graph"),
        P(("groups", "pipe"), "graph"),
        P(),
        P(),
        P(None, "feat"),
        P("feat", None),
    )
    out_specs = (
        P(("groups", "pipe"), "graph", None),
        P(("groups", "pipe"), "graph", None),
        P(("groups", "pipe"), "graph", None),
    )
    return jax.shard_map(
        on_device, mesh=mesh, in_specs=in_specs, out_specs=out_specs, check_vma=False
    )
```

profile of v0, /device:TPU:1, one launch (start us, length us, event | category | flops | bytes accessed | tf_op | source)
XLA Modules:
  0.0 132.7 jit_solution(10445453874940953759)
XLA Ops:
  8.7 1.1 constant_dynamic-update-slice_fusion.1
  10.5 11.9 %all_gather.16 = bf16[32,1536]{1,0:T(8,128)(2,1)S(1)} all-gather(bf16[8,1536]{1,0:T(8,128)(2,1)S(1)} %pad_maximum_fusion.2), channel_id=1, replica_groups=mesh['groups'=2,'graph'=4,'pipe'=2,'feat'=2] {'graph'}, dimensions={0}, use_global_device_ids=true | all-gather | bytes 122880 | tf_op jit(solution)/shard_map/all_gather | solution.py:94
  22.4 10.2 %all_gather.15 = bf16[32,1024]{1,0:T(8,128)(2,1)S(1)} all-gather(bf16[8,1024]{1,0:T(8,128)(2,1)S(1)} %pad_maximum_fusion.3), channel_id=1, replica_groups=mesh['groups'=2,'graph'=4,'pipe'=2,'feat'=2] {'graph'}, dimensions={0}, use_global_device_ids=true | all-gather | bytes 81920 | tf_op jit(solution)/shard_map/all_gather | solution.py:93
  33.7 1.6 %broadcast_in_dim.27 = f32[512,1024]{1,0:T(8,128)} broadcast(f32[]{:T(128)} %constant.5.clone.1), dimensions={} | broadcast | bytes 2097156 | tf_op jit(solution)/shard_map/broadcast_in_dim | solution.py:77
  35.3 3.9 %while.22 = (s32[]{:T(128)}, f32[512,1024]{1,0:T(8,128)}, f32[512,1536]{1,0:T(8,128)S(1)}, s32[]{:T(128)}, s32[512]{0:T(512)S(1)}, /*index=5*/bf16[32,1024]{1,0:...) while((s32[]{:T(128)}, f32[512,1024]{1,0:T(8,128)}, ...), condition=%wide.region_1.0_spmd, body=%wide.region_0.0_spmd.sunk | while | flops 21307396 | bytes 2788531 | solution.py:41
  36.5 2.1 %fusion.114 = f32[512,1024]{1,0:T(8,128)} fusion(f32[512,1024]{1,0:T(8,128)} %get-tuple-element.237, s32[]{:T(128)S(6)} %select_n.15, bf16[32,1024]{1,0:T(8,128)(2,1)S(1)} %get-tuple-element.253, s32[128]{0:T(128)S(1)} %dynamic_slice.77), kind=kOutput, calls=%fused_computation.3.clone.1 | convolution fusion | flops 8523776 | bytes 1114628 | tf_op jit(solution)/shard_map/while/body/dot_general | solution.py:22
  39.5 3.7 %fusion.36 = (f32[512,512]{1,0:T(8,128)}, f32[512,512]{1,0:T(8,128)}, f32[512,512]{1,0:T(8,128)}) fusion(f32[512,1536]{1,0:T(8,128)S(1)} %get-tuple-element.86, f32[512,1024]{1,0:T(8,128)} %get-tuple-element.85, bf16[1,512,512]{2,1,0:T(8,128)(2,1)} %param.21), kind=kLoop, calls=%fused_computation.57 | loop fusion | flops 1048576 | bytes 8912896 | tf_op jit(solution)/shard_map/add | solution.py:101
  43.2 2.5 %fusion.19 = bf16[256,1024]{1,0:T(8,128)(2,1)S(1)} fusion(f32[512,512]{1,0:T(8,128)} %get-tuple-element.122, f32[512,512]{1,0:T(8,128)} %get-tuple-element.121, s32[]{:T(128)S(6)} %select_n.12, s32[256]{0:T(256)S(1)} %bitcast.47, pred[256,512]{1,0:T(32,128)(4,1)S(1)} %iota_compare_fusion.12, bf16[256]{0:T(256)(128)(2,1)S(1)} %reduce), kind=kOutput, calls=%fused_computation.36 | convolution fusion | flops 404946944 | bytes 4786688 | tf_op jit(solution)/shard_map/te,tc->ec/dot_general | solution.py:124
  45.8 2.8 %fusion.56 = f32[256,1024]{1,0:T(8,128)} fusion(bf16[512,1024]{1,0:T(8,128)(2,1)} %all-gather.4.cloned.1.call-done, bf16[256,1024]{1,0:T(8,128)(2,1)S(1)} %fusion.19), kind=kOutput, calls=%fused_computation.78 | convolution fusion | flops 268435456 | bytes 2359296 | tf_op jit(solution)/shard_map/dot_general | solution.py:128
  48.6 1.8 %fusion.51 = f32[256,1024]{1,0:T(8,128)S(1)} fusion(bf16[1024,512]{1,0:T(8,128)(2,1)} %all-gather.6.cloned.1.call-done, f32[512,512]{1,0:T(8,128)S(1)} %copy-done.5, s32[]{:T(128)S(6)} %select_n.12, f32[256]{0:T(256)S(1)} %dynamic-slice), kind=kOutput, calls=%fused_computation.75 | convolution fusion | flops 268697600 | bytes 2622468 | tf_op jit(solution)/shard_map/ed,hd->eh/dot_general | solution.py:133
  50.4 1.0 copy-done.11
  51.4 1.4 %fusion.48 = f32[256,512]{1,0:T(8,128)} fusion(bf16[512,1024]{1,0:T(8,128)(2,1)S(1)} %copy-done.7, f32[256,1024]{1,0:T(8,128)S(1)} %fusion.51, f32[256,1024]{1,0:T(8,128)S(1)} %copy-done.8), kind=kOutput, calls=%fused_computation.74 | convolution fusion | flops 270794752 | bytes 3670016 | tf_op jit(solution)/shard_map/eh,dh->ed/dot_general | solution.py:138
  52.8 3.1 %fusion.21 = f32[256,512]{1,0:T(8,128)} fusion(bf16[512,1024]{1,0:T(8,128)(2,1)S(1)} %copy-done.7, f32[256,1024]{1,0:T(8,128)} %copy-done.11, f32[256,1024]{1,0:T(8,128)S(1)} %copy-done.9, bf16[256,1024]{1,0:T(8,128)(2,1)S(1)} %fusion.19), kind=kOutput, calls=%fused_computation.39 | convolution fusion | flops 540278784 | bytes 4980736 | tf_op jit(solution)/shard_map/eh,dh->ed/dot_general | solution.py:139
  55.9 2.4 %pad_maximum_fusion.1 = f32[256,1024]{1,0:T(8,128)} fusion(f32[256,512]{1,0:T(8,128)} %fusion.21, f32[256,512]{1,0:T(8,128)} %fusion.48), kind=kLoop, calls=%fused_computation.55 | loop fusion | flops 262144 | bytes 2097152 | tf_op jit(solution)/shard_map/concatenate | solution.py:141
  59.1 25.8 %all-gather.8.cloned.1.call-done = f32[512,1024]{1,0:T(8,128)} async-done(((f32[256,1024]{1,0:T(8,128)}), f32[512,1024]{1,0:T(8,128)}) %all-gather.8.cloned.1.call-update) | async-done | bytes 2097168 | tf_op jit(solution)/shard_map/all_gather | solution.py:140
  84.9 3.0 %fusion.17 = bf16[512,1024]{1,0:T(8,128)(2,1)S(1)} fusion(f32[512,1024]{1,0:T(8,128)} %all-gather.8.cloned.1.call-done, bf16[512]{0:T(512)(128)(2,1)S(1)} %fusion.75, s32[256]{0:T(256)S(1)} %bitcast.48, bf16[256]{0:T(256)(128)(2,1)S(1)} %reduce, s32[256]{0:T(256)S(1)} %bitcast.50), kind=kOutput, calls=%fused_computation.30 | convolution fusion | flops 541196288 | bytes 3149312 | tf_op jit(solution)/shard_map/te,tc->ec/dot_general | solution.py:150
  87.9 2.5 %while.23 = (s32[]{:T(128)}, f32[32,2560]{1,0:T(8,128)S(1)}, s32[]{:T(128)}, s32[512]{0:T(512)S(1)}, f32[512,512]{1,0:T(8,128)S(1)}, /*index=5*/s32[512]{0:T(512...) while((s32[]{:T(128)}, f32[32,2560]{1,0:T(8,128)S(1)}, ...), condition=%wide.region_3.0_spmd, body=%wide.region_2.0_spmd.sunk | while | flops 42201092 | bytes 2100911 | solution.py:171
  90.4 0.7 copy-done.1
  91.2 23.8 %reduce-scatter.2.cloned.1.call-done = f32[8,2560]{1,0:T(8,128)} async-done(((f32[32,2560]{1,0:T(8,128)}), f32[8,2560]{1,0:T(8,128)}) %reduce-scatter.2.cloned.1.call-update) | async-done | bytes 81936 | tf_op jit(solution)/shard_map/reduce_scatter | solution.py:170
  115.0 1.2 fusion.66
  116.3 1.2 fusion.69
  117.5 1.2 fusion.24
  118.7 1.2 fusion.25
  120.0 6.2 %all-reduce = (bf16[8,512]{1,0:T(8,128)(2,1)}, f32[1,8,512]{2,1,0:T(8,128)}, f32[1,8,512]{2,1,0:T(8,128)}) all-reduce(f32[8,512]{1,0:T(8,128)S(1)} %slice-done, f32[1,8,512]{2,1,0:T(8,128)S(1)} %fusion.25, f32[1,8,512]{2,1,0:T(8,128)S(1)} %fusion.24), channel_id=1, replica_groups=mesh['groups'=2,'graph'=4,'pipe'=2,'feat'=2] {'feat'}, use_global_device_ids=true, to_apply=%region_5.0 | all-reduce | flops 12288 | bytes 90112 | tf_op jit(solution)/shard_map/psum | solution.py:192
  (73 shorter events, 5.0 us)
Async XLA Ops:
  7.2 2.8 %copy-start = (bf16[1,8,512]{2,1,0:T(8,128)(2,1)S(1)}, bf16[1,8,512]{2,1,0:T(8,128)(2,1)}, u32[]{:S(2)}) copy-start(bf16[1,8,512]{2,1,0:T(8,128)(2,1)} %param.18) | copy-start | bytes 24580
  7.2 2.7 %copy-start.3 = (bf16[512,512]{1,0:T(8,128)(2,1)S(1)}, bf16[512,512]{1,0:T(8,128)(2,1)}, u32[]{:S(2)}) copy-start(bf16[512,512]{1,0:T(8,128)(2,1)} %param.29) | copy-start | bytes 1572868
  7.2 3.0 %copy-start.12 = (bf16[1,8,512]{2,1,0:T(8,128)(2,1)S(1)}, bf16[1,8,512]{2,1,0:T(8,128)(2,1)}, u32[]{:S(2)}) copy-start(bf16[1,8,512]{2,1,0:T(8,128)(2,1)} %param.19) | copy-start | bytes 24580
  7.2 38.6 %all-gather.4.cloned.1.call-start = ((), (), s32[]{:S(2)}) async-start(), calls=%async_computation.1 | async-start | bytes 1572864 | tf_op jit(solution)/shard_map/all_gather | solution.py:117
  7.9 40.7 %all-gather.6.cloned.1.call-start = ((), (), s32[]{:S(2)}) async-start(), calls=%async_computation.2 | async-start | bytes 1572864 | tf_op jit(solution)/shard_map/all_gather | solution.py:118
  8.7 76.2 %all-gather.8.cloned.1.call-start = ((), (), s32[]{:S(2)}) async-start(), calls=%async_computation.3 | async-start | bytes 3145728 | tf_op jit(solution)/shard_map/all_gather | solution.py:140
  8.7 1.7 %copy-start.13 = (bf16[1,8,512]{2,1,0:T(8,128)(2,1)S(1)}, bf16[1,8,512]{2,1,0:T(8,128)(2,1)}, u32[]{:S(2)}) copy-start(bf16[1,8,512]{2,1,0:T(8,128)(2,1)} %param.20) | copy-start | bytes 24580
  33.3 2.0 %copy-start.17 = (s32[1,512]{1,0:T(1,128)S(1)}, s32[1,512]{1,0:T(1,128)}, u32[]{:S(2)}) copy-start(s32[1,512]{1,0:T(1,128)} %param.22) | copy-start | bytes 6148
  33.3 2.0 %copy-start.18 = (s32[1,512]{1,0:T(1,128)S(1)}, s32[1,512]{1,0:T(1,128)}, u32[]{:S(2)}) copy-start(s32[1,512]{1,0:T(1,128)} %param.23) | copy-start | bytes 6148
  35.3 4.0 %copy-start.16 = (bf16[1,256]{1,0:T(2,128)(2,1)S(1)}, bf16[1,256]{1,0:T(2,128)(2,1)}, u32[]{:S(2)}) copy-start(bf16[1,256]{1,0:T(2,128)(2,1)} %param.27) | copy-start | bytes 1540
  35.3 4.1 %copy-start.15 = (s32[1,256]{1,0:T(1,128)S(1)}, s32[1,256]{1,0:T(1,128)}, u32[]{:S(2)}) copy-start(s32[1,256]{1,0:T(1,128)} %param.26) | copy-start | bytes 3076
  39.5 3.7 %copy-start.14 = (s32[1,256]{1,0:T(1,128)S(1)}, s32[1,256]{1,0:T(1,128)}, u32[]{:S(2)}) copy-start(s32[1,256]{1,0:T(1,128)} %param.25) | copy-start | bytes 3076
  45.7 2.9 %copy-start.5 = (f32[512,512]{1,0:T(8,128)S(1)}, f32[512,512]{1,0:T(8,128)}, u32[]{:S(2)}) copy-start(f32[512,512]{1,0:T(8,128)} %get-tuple-element.123) | copy-start | bytes 3145732
  45.8 5.6 %copy-start.7 = (bf16[512,1024]{1,0:T(8,128)(2,1)S(1)}, bf16[512,1024]{1,0:T(8,128)(2,1)}, u32[]{:S(2)}) copy-start(bf16[512,1024]{1,0:T(8,128)(2,1)} %all-gather.4.cloned.1.call-done) | copy-start | bytes 3145732
  48.6 2.8 %copy-start.8 = (f32[256,1024]{1,0:T(8,128)S(1)}, f32[256,1024]{1,0:T(8,128)}, u32[]{:S(2)}) copy-start(f32[256,1024]{1,0:T(8,128)} %fusion.56) | copy-start | bytes 3145732
  50.4 1.0 copy-start.11
  51.4 1.4 %copy-start.9 = (f32[256,1024]{1,0:T(8,128)S(1)}, f32[256,1024]{1,0:T(8,128)}, u32[]{:S(2)}) copy-start(f32[256,1024]{1,0:T(8,128)} %fusion.56) | copy-start | bytes 3145732
  55.9 2.6 %copy-start.6 = (bf16[1024,512]{1,0:T(8,128)(2,1)S(1)}, bf16[1024,512]{1,0:T(8,128)(2,1)}, u32[]{:S(2)}) copy-start(bf16[1024,512]{1,0:T(8,128)(2,1)} %all-gather.6.cloned.1.call-done) | copy-start | bytes 3145732
  55.9 2.7 %copy-start.10 = (f32[256,1024]{1,0:T(8,128)S(1)}, f32[256,1024]{1,0:T(8,128)}, u32[]{:S(2)}) copy-start(f32[256,1024]{1,0:T(8,128)} %fusion.56) | copy-start | bytes 3145732
  58.4 56.7 %reduce-scatter.2.cloned.1.call-start = ((), (), s32[]{:S(2)}) async-start(), calls=%async_computation.4 | async-start | bytes 409600 | tf_op jit(solution)/shard_map/reduce_scatter | solution.py:170
  87.9 27.1 %copy-start.2 = (bf16[512,512]{1,0:T(8,128)(2,1)S(1)}, bf16[512,512]{1,0:T(8,128)(2,1)}, u32[]{:S(2)}) copy-start(bf16[512,512]{1,0:T(8,128)(2,1)} %param.28) | copy-start | bytes 1572868
  87.9 29.6 %copy-start.4 = (bf16[512,512]{1,0:T(8,128)(2,1)S(1)}, bf16[512,512]{1,0:T(8,128)(2,1)}, u32[]{:S(2)}) copy-start(bf16[512,512]{1,0:T(8,128)(2,1)} %param.29) | copy-start | bytes 1572868
  90.4 0.7 copy-start.1
  115.0 5.0 %slice-start = ((f32[8,2560]{1,0:T(8,128)}), f32[8,512]{1,0:T(8,128)S(1)}, s32[]{:S(2)}) async-start(f32[8,2560]{1,0:T(8,128)} %reduce-scatter.2.cloned.1.call-done), calls=%async_computation.5 | async-start | bytes 32768 | tf_op jit(solution)/shard_map/slice | solution.py:183
Sparse Core Ops, SparseCore 0:
  9.6 11.4 all-gather.3
  22.6 10.1 all-gather.5
  58.5 26.3 all-gather.7
  91.3 23.6 reduce-scatter.1
where the time goes:
time: 134 us; the launch traced here: 133 us
  waiting for transfers between devices  51.1 us (38%)
  blocking collectives  28.3 us (21%)
  matrix products  23.8 us (18%)
  between operations  14.7 us (11%)
  other arithmetic  6.37 us (5%)
  local copies, waits for them, and re-layouts  5.44 us (4%)
  loops' own time  2.77 us (2%)
    all_gather x1, waiting for transfers between devices, on_device(): lax.all_gather(jnp.concatenate([part_cot, part_tan], axis=1), 'feat', axi...  25.8 us
    reduce_scatter x1, waiting for transfers between devices, on_device(): lax.psum_scatter(lax.fori_loop(0, valid_blocks, atom_one_block, jnp.zeros...  23.8 us
    all_gather x1, blocking collectives, on_device(): lax.all_gather(tgt_rows, 'graph', axis=0, tiled=True)  11.9 us
    all_gather x1, blocking collectives, on_device(): lax.all_gather(src_rows, 'graph', axis=0, tiled=True)  10.2 us
    psum x1, blocking collectives, on_device(): lax.psum((update_part, grad_part, hvp_part), 'feat')  6.16 us
    dot_general x4, matrix products, project_cols(): jnp.einsum('ac,kc->ak', values, weight_cols.astype(jnp.float32), precisio...  4.94 us
    add x1, other arithmetic, on_device(): edge_state[0].astype(jnp.float32) + sel_src[:, :emb_width]  3.7 us
    dot_general x1, matrix products, on_device(): jnp.einsum('eh,dh->ed', tan_hid_cot, weight_in, preferred_element_type=jn...  3.11 us
  transfers between devices with their start and end apart: 4, of which 2 were waited for; matrix products, arithmetic and copies ran while one was open for 12% of the time, Pallas kernels for 0%

commit v1 on v0

v1 whole, which is shorter than its diff:
```python
import functools

import jax
import jax.numpy as jnp
from jax import lax
from jax.experimental import pallas as pl
from jax.experimental.pallas import tpu as pltpu
from jax.sharding import PartitionSpec as P

EBLOCK = 128
F32 = jnp.float32
BF16 = jnp.bfloat16
MESH = pl.DeviceIdType.MESH


def mm(a, b):
    return jnp.dot(a, b, preferred_element_type=F32)


def mm_nt(a, b):
    return lax.dot_general(a, b, (((1,), (1,)), ((), ())), preferred_element_type=F32)


def as_column(row):
    return jnp.transpose(jnp.broadcast_to(row, (8, row.shape[1])))[:, :1]


def split_rows(x):
    high = x.astype(BF16)
    return jnp.concatenate([high, (x - high.astype(F32)).astype(BF16)], axis=0)


def join_rows(x):
    half = x.shape[0] // 2
    return x[:half] + x[half:]


def kernel(
    n,
    state_ref,
    dir_ref,
    up_ref,
    src_ref,
    tgt_ref,
    blocks_ref,
    tin_ref,
    tout_ref,
    coef_ref,
    edge_hbm,
    wsrc_hbm,
    wtgt_hbm,
    win_hbm,
    wout_hbm,
    upd_out,
    grad_out,
    hvp_out,
    edge_v,
    wsrc_v,
    wtgt_v,
    win_v,
    wout_v,
    stage,
    gathered,
    upd_own,
    upd_send,
    upd_recv,
    cot_own,
    cot_send,
    cot_recv,
    pair_send,
    pair_recv,
    load_sem,
    g_send,
    g_recv,
    u_send,
    u_recv,
    c_send,
    c_recv,
    p_send,
    p_recv,
):
    me = lax.axis_index("graph")
    other = 1 - lax.axis_index("feat")
    atoms = state_ref.shape[1]
    width = state_ref.shape[2]
    all_atoms = n * atoms
    slots = src_ref.shape[1]
    trips = tin_ref.shape[1]
    half = width // 2

    loads = []
    for i, (s, d) in enumerate(
        (
            (edge_hbm.at[0], edge_v),
            (win_hbm, win_v),
            (wout_hbm, wout_v),
            (wsrc_hbm, wsrc_v),
            (wtgt_hbm, wtgt_v),
        )
    ):
        c = pltpu.make_async_copy(s, d, load_sem.at[i])
        c.start()
        loads.append(c)

    barrier = pltpu.get_barrier_semaphore()
    for k in range(1, n):
        pl.semaphore_signal(
            barrier, inc=1, device_id={"graph": lax.rem(me + k, n)}, device_id_type=MESH
        )
    pl.semaphore_signal(barrier, inc=1, device_id={"feat": other}, device_id_type=MESH)

    up = up_ref[0].astype(F32)
    mine = jnp.concatenate(
        [
            jnp.concatenate([state_ref[0].astype(F32), up[:, :half]], axis=1),
            jnp.concatenate([dir_ref[0].astype(F32), up[:, half:]], axis=1),
        ],
        axis=0,
    ).astype(BF16)
    stage[...] = mine
    gathered[me] = mine
    pl.semaphore_wait(barrier, n)

    gathers = []
    for k in range(1, n):
        c = pltpu.make_async_remote_copy(
            src_ref=stage,
            dst_ref=gathered.at[me],
            send_sem=g_send.at[k - 1],
            recv_sem=g_recv.at[k - 1],
            device_id={"graph": lax.rem(me + k, n)},
            device_id_type=MESH,
        )
        c.start()
        gathers.append(c)

    src_col = as_column(src_ref[...])
    tgt_row = tgt_ref[...]
    tgt_col = as_column(tgt_row)
    used = blocks_ref[0, 0] * EBLOCK
    pair = 2 * all_atoms
    lane = lax.broadcasted_iota(jnp.int32, (slots, 3 * pair), 1)
    base = jnp.where(lane >= 2 * pair, lane - 2 * pair, jnp.where(lane >= pair, lane - pair, lane))
    hot = ((base == src_col) | (base == tgt_col + all_atoms)).astype(F32)
    lane2 = lax.broadcasted_iota(jnp.int32, (slots, pair), 1)
    row2 = lax.broadcasted_iota(jnp.int32, (slots, pair), 0)
    tgt_hot = (
        ((lane2 == tgt_col) | (lane2 == tgt_col + all_atoms)) & (row2 < used)
    ).astype(F32).astype(BF16)
    atom_iota = lax.broadcasted_iota(jnp.int32, (all_atoms, slots), 0)
    slot_iota = lax.broadcasted_iota(jnp.int32, (all_atoms, slots), 1)
    tgt_hot_t = ((atom_iota == tgt_row) & (slot_iota < used)).astype(F32).astype(BF16)
    in_hot = (
        (lax.broadcasted_iota(jnp.int32, (trips, slots), 1) == as_column(tin_ref[...]))
        .astype(F32)
        .astype(BF16)
    )
    out_weighted = jnp.where(
        lax.broadcasted_iota(jnp.int32, (slots, trips), 0) == tout_ref[...],
        coef_ref[...].astype(F32),
        0.0,
    ).astype(BF16)
    hops = mm(in_hot, hot.astype(BF16)).astype(BF16)
    spread = hot + mm(out_weighted, hops)
    spread_high = spread.astype(BF16).astype(F32)
    spread_low = spread - spread_high
    spread_split = jnp.where((lane >= pair) & (lane < 2 * pair), spread_low, spread_high)
    spread_t = jnp.transpose(spread_split[:, : 2 * pair]).astype(BF16)
    spread_split = spread_split.astype(BF16)

    loads[0].wait()
    picked = mm(in_hot, edge_v[...]).astype(BF16)
    mixed = edge_v[...].astype(F32) + mm(out_weighted, picked)
    loads[1].wait()
    hidden_edge = mm(mixed.astype(BF16), win_v[...])
    for c in loads[2:]:
        c.wait()

    for c in gathers:
        c.wait_recv()
    rows = gathered[...].astype(F32)
    state = rows[:, :atoms, :width].reshape(all_atoms, width)
    direction = rows[:, atoms:, :width].reshape(all_atoms, width)
    upstream = jnp.concatenate(
        [
            rows[:, :atoms, width:].reshape(all_atoms, half),
            rows[:, atoms:, width:].reshape(all_atoms, half),
        ],
        axis=1,
    ).astype(BF16)
    both = jnp.concatenate([state, direction], axis=0).astype(BF16)
    proj_src = mm(both, wsrc_v[...])
    proj_tgt = mm(both, wtgt_v[...])
    proj = jnp.concatenate(
        [
            proj_src[:all_atoms],
            proj_tgt[:all_atoms],
            proj_src[all_atoms:],
            proj_tgt[all_atoms:],
        ],
        axis=0,
    ).astype(BF16)
    proj_hidden = mm(proj, win_v[...])
    high = proj_hidden.astype(BF16)
    low = (proj_hidden - high.astype(F32)).astype(BF16)
    hidden_pre = hidden_edge + mm(
        spread_split, jnp.concatenate([high[:pair], high[:pair], low[:pair]], axis=0)
    )
    tan_hidden = mm(
        spread_split, jnp.concatenate([high[pair:], high[pair:], low[pair:]], axis=0)
    )
    act_cot = mm(tgt_hot, split_rows(mm_nt(upstream, wout_v[...])))

    sig = jax.nn.sigmoid(hidden_pre)
    activation = (hidden_pre * sig).astype(BF16)
    rest = 1.0 - sig
    first_slope = sig * (1.0 + hidden_pre * rest)
    second_slope = sig * rest * (2.0 + hidden_pre * (1.0 - 2.0 * sig))
    hid_cot = (act_cot * first_slope).astype(BF16)
    tan_hid_cot = (act_cot * second_slope * tan_hidden).astype(BF16)

    update = join_rows(mm(split_rows(mm(tgt_hot_t, activation)), wout_v[...]))
    for p in range(n):
        part = update[p * atoms : (p + 1) * atoms]
        packed = jnp.concatenate([part[:, :half], part[:, half:]], axis=0)
        upd_own[p] = packed
        upd_send[p] = packed.astype(BF16)
    updates = []
    for k in range(1, n):
        peer = lax.rem(me + k, n)
        c = pltpu.make_async_remote_copy(
            src_ref=upd_send.at[peer],
            dst_ref=upd_recv.at[k - 1],
            send_sem=u_send.at[k - 1],
            recv_sem=u_recv.at[k - 1],
            device_id={"graph": peer},
            device_id_type=MESH,
        )
        c.start()
        updates.append(c)

    via = jnp.concatenate(
        [join_rows(mm(spread_t, hid_cot)), join_rows(mm(spread_t, tan_hid_cot))], axis=0
    )
    via = join_rows(mm_nt(split_rows(via), win_v[...]))
    via_src = jnp.concatenate([via[:all_atoms], via[pair : pair + all_atoms]], axis=0)
    via_tgt = jnp.concatenate([via[all_atoms:pair], via[pair + all_atoms :]], axis=0)
    grads = join_rows(
        mm_nt(split_rows(via_src), wsrc_v[...]) + mm_nt(split_rows(via_tgt), wtgt_v[...])
    )
    for p in range(n):
        packed = jnp.concatenate(
            [
                grads[p * atoms : (p + 1) * atoms],
                grads[all_atoms + p * atoms : all_atoms + (p + 1) * atoms],
            ],
            axis=0,
        )
        cot_own[p] = packed
        cot_send[p] = packed.astype(BF16)
    cots = []
    for k in range(1, n):
        peer = lax.rem(me + k, n)
        c = pltpu.make_async_remote_copy(
            src_ref=cot_send.at[peer],
            dst_ref=cot_recv.at[k - 1],
            send_sem=c_send.at[k - 1],
            recv_sem=c_recv.at[k - 1],
            device_id={"graph": peer},
            device_id_type=MESH,
        )
        c.start()
        cots.append(c)

    upd_sum = upd_own[me]
    for k in range(1, n):
        updates[k - 1].wait_recv()
        upd_sum = upd_sum + upd_recv[k - 1].astype(F32)
    cot_sum = cot_own[me]
    for k in range(1, n):
        cots[k - 1].wait_recv()
        cot_sum = cot_sum + cot_recv[k - 1].astype(F32)
    total = jnp.concatenate([cot_sum, upd_sum], axis=1)
    pair_send[...] = total
    c = pltpu.make_async_remote_copy(
        src_ref=pair_send,
        dst_ref=pair_recv,
        send_sem=p_send,
        recv_sem=p_recv,
        device_id={"feat": other},
        device_id_type=MESH,
    )
    c.start()
    c.wait_recv()
    total = total + pair_recv[...]
    grad_out[0] = total[:atoms, :width]
    hvp_out[0] = total[atoms:, :width]
    upd_out[0] = jnp.concatenate([total[:atoms, width:], total[atoms:, width:]], axis=1).astype(
        BF16
    )
    c.wait_send()
    for c in gathers + updates + cots:
        c.wait_send()


def on_device(
    atom_state,
    direction,
    upstream,
    edge_state,
    edge_src,
    edge_tgt,
    edge_blocks,
    trip_in,
    trip_out,
    trip_coef,
    w_src,
    w_tgt,
    w_in,
    w_out,
):
    n = lax.axis_size("graph")
    atoms, width = atom_state.shape[1:]
    slots = edge_state.shape[1]
    hidden = w_in.shape[1]
    half = width // 2
    vmem = pl.BlockSpec(memory_space=pltpu.VMEM)
    smem = pl.BlockSpec(memory_space=pltpu.SMEM)
    far = pl.BlockSpec(memory_space=pl.ANY)
    dma = pltpu.SemaphoreType.DMA
    return pl.pallas_call(
        functools.partial(kernel, n),
        name="interaction",
        out_shape=(
            jax.ShapeDtypeStruct((1, atoms, width), BF16),
            jax.ShapeDtypeStruct((1, atoms, width), F32),
            jax.ShapeDtypeStruct((1, atoms, width), F32),
        ),
        in_specs=[vmem] * 5 + [smem] + [vmem] * 3 + [far] * 5,
        out_specs=(vmem, vmem, vmem),
        scratch_shapes=[
            pltpu.VMEM((slots, width), BF16),
            pltpu.VMEM((width, width), BF16),
            pltpu.VMEM((width, width), BF16),
            pltpu.VMEM((width, hidden), BF16),
            pltpu.VMEM((hidden, width), BF16),
            pltpu.VMEM((2 * atoms, width + half), BF16),
            pltpu.VMEM((n, 2 * atoms, width + half), BF16),
            pltpu.VMEM((n, 2 * atoms, half), F32),
            pltpu.VMEM((n, 2 * atoms, half), BF16),
            pltpu.VMEM((n - 1, 2 * atoms, half), BF16),
            pltpu.VMEM((n, 2 * atoms, width), F32),
            pltpu.VMEM((n, 2 * atoms, width), BF16),
            pltpu.VMEM((n - 1, 2 * atoms, width), BF16),
            pltpu.VMEM((2 * atoms, width + half), F32),
            pltpu.VMEM((2 * atoms, width + half), F32),
            dma((5,)),
            dma((n - 1,)),
            dma((n - 1,)),
            dma((n - 1,)),
            dma((n - 1,)),
            dma((n - 1,)),
            dma((n - 1,)),
            dma,
            dma,
        ],
        compiler_params=pltpu.CompilerParams(
            collective_id=0, has_side_effects=True, vmem_limit_bytes=48 * 1024 * 1024
        ),
    )(
        atom_state,
        direction,
        upstream,
        edge_src,
        edge_tgt,
        edge_blocks,
        trip_in,
        trip_out,
        trip_coef,
        edge_state,
        w_src,
        w_tgt,
        w_in,
        w_out,
    )


def solution(mesh):
    in_specs = (
        P(("groups", "pipe"), "graph", None),
        P(("groups", "pipe"), "graph", None),
        P(("groups", "pipe"), "graph", None),
        P(("groups", "pipe"), "graph", None),
        P(("groups", "pipe"), "graph"),
        P(("groups", "pipe"), "graph"),
        P(("groups", "pipe"), "graph"),
        P(("groups", "pipe"), "graph"),
        P(("groups", "pipe"), "graph"),
        P(("groups", "pipe"), "graph"),
        P(),
        P(),
        P(None, "feat"),
        P("feat", None),
    )
    out_specs = (
        P(("groups", "pipe"), "graph", None),
        P(("groups", "pipe"), "graph", None),
        P(("groups", "pipe"), "graph", None),
    )
    return jax.shard_map(
        on_device, mesh=mesh, in_specs=in_specs, out_specs=out_specs, check_vma=False
    )
```

time: 134 us -> 30.8 us (0.23)
  the two profiles are of different devices: /device:TPU:1 before, /device:TPU:0 now
where the time goes in v1:
time: 30.8 us; the launch traced here: 30.2 us
  Pallas kernels  17 us (55%)
  local copies, waits for them, and re-layouts  11.8 us (38%)
  between operations  1.33 us (4%)
    pallas_call x1, Pallas kernels, on_device(): pl.pallas_call(functools.partial(kernel, n), name='interaction', out_shap...  17 us
    unnamed x29, local copies, waits for them, and re-layouts  11.8 us

profile of v1, /device:TPU:0, one launch (start us, length us, event | category | flops | bytes accessed | tf_op | source)
XLA Modules:
  0.0 30.2 jit_solution(5826769073931586539)
XLA Ops:
  0.6 0.0 copy-start.10
  1.3 0.0 copy-done.10
  1.3 1.0 %copy-done = bf16[1,512,512]{2,1,0:T(8,128)(2,1)S(1)} copy-done((bf16[1,512,512]{2,1,0:T(8,128)(2,1)S(1)}, bf16[1,512,512]{2,1,0:T(8,128)(2,1)}, u32[]{:S(2)}) %copy-start) | copy-done | bytes 524312
  2.4 0.0 copy-start.1
  2.4 1.0 %copy-done.1 = bf16[512,512]{1,0:T(8,128)(2,1)S(1)} copy-done((bf16[512,512]{1,0:T(8,128)(2,1)S(1)}, bf16[512,512]{1,0:T(8,128)(2,1)}, u32[]{:S(2)}) %copy-start.1) | copy-done | bytes 524312
  3.4 0.0 copy-start.2
  3.4 1.0 %copy-done.2 = bf16[512,512]{1,0:T(8,128)(2,1)S(1)} copy-done((bf16[512,512]{1,0:T(8,128)(2,1)S(1)}, bf16[512,512]{1,0:T(8,128)(2,1)}, u32[]{:S(2)}) %copy-start.2) | copy-done | bytes 524312
  4.4 0.0 copy-start.3
  4.4 1.0 %copy-done.3 = bf16[512,512]{1,0:T(8,128)(2,1)S(1)} copy-done((bf16[512,512]{1,0:T(8,128)(2,1)S(1)}, bf16[512,512]{1,0:T(8,128)(2,1)}, u32[]{:S(2)}) %copy-start.3) | copy-done | bytes 524312
  5.5 0.0 copy-start.4
  5.5 1.0 %copy-done.4 = bf16[512,512]{1,0:T(8,128)(2,1)S(1)} copy-done((bf16[512,512]{1,0:T(8,128)(2,1)S(1)}, bf16[512,512]{1,0:T(8,128)(2,1)}, u32[]{:S(2)}) %copy-start.4) | copy-done | bytes 524312
  6.5 0.0 copy-start.5
  6.5 0.7 %copy-done.5 = bf16[1,8,512]{2,1,0:T(8,128)(2,1)S(1)} copy-done((bf16[1,8,512]{2,1,0:T(8,128)(2,1)S(1)}, bf16[1,8,512]{2,1,0:T(8,128)(2,1)}, u32[]{:S(2)}) %copy-start.5) | copy-done | bytes 8216
  7.2 0.0 copy-start.6
  7.2 0.7 %copy-done.6 = bf16[1,8,512]{2,1,0:T(8,128)(2,1)S(1)} copy-done((bf16[1,8,512]{2,1,0:T(8,128)(2,1)S(1)}, bf16[1,8,512]{2,1,0:T(8,128)(2,1)}, u32[]{:S(2)}) %copy-start.6) | copy-done | bytes 8216
  7.9 0.7 %copy-done.7 = bf16[1,8,512]{2,1,0:T(8,128)(2,1)S(1)} copy-done((bf16[1,8,512]{2,1,0:T(8,128)(2,1)S(1)}, bf16[1,8,512]{2,1,0:T(8,128)(2,1)}, u32[]{:S(2)}) %copy-start.7) | copy-done | bytes 8216
  8.6 0.7 %copy-done.8 = s32[1,512]{1,0:T(1,128)S(1)} copy-done((s32[1,512]{1,0:T(1,128)S(1)}, s32[1,512]{1,0:T(1,128)}, u32[]{:S(2)}) %copy-start.8) | copy-done | bytes 2072
  9.3 0.7 %copy-done.9 = s32[1,512]{1,0:T(1,128)S(1)} copy-done((s32[1,512]{1,0:T(1,128)S(1)}, s32[1,512]{1,0:T(1,128)}, u32[]{:S(2)}) %copy-start.9) | copy-done | bytes 2072
  10.0 0.7 %copy-done.11 = s32[1,256]{1,0:T(1,128)S(1)} copy-done((s32[1,256]{1,0:T(1,128)S(1)}, s32[1,256]{1,0:T(1,128)}, u32[]{:S(2)}) %copy-start.11) | copy-done | bytes 1048
  10.7 0.7 %copy-done.12 = bf16[1,256]{1,0:T(2,128)(2,1)S(1)} copy-done((bf16[1,256]{1,0:T(2,128)(2,1)S(1)}, bf16[1,256]{1,0:T(2,128)(2,1)}, u32[]{:S(2)}) %copy-start.12) | copy-done | bytes 536
  11.3 17.0 %interaction.1 = (bf16[1,8,512]{2,1,0:T(8,128)(2,1)S(1)}, f32[1,8,512]{2,1,0:T(8,128)S(1)}, f32[1,8,512]{2,1,0:T(8,128)S(1)}) custom-call(bf16[1,8,512]{2,1,0:T(8,128)(2,1)S(1)} %copy-done.5, bf16[1,8,512]{2,1,0:T(8,128)(2,1)S(1)} %copy-done.6, bf16[1,8,512]{2,1,0:T(8,128)(2,1)S(1)} %copy-done.7, s32[1,512]{1,0:T(1,128)S(1)} %copy-done.8, ...), custom_call_target="tpu_custom_call" | custom-call | tf_op jit(solution)/shard_map/interaction/pallas_call | solution.py:331
  28.4 0.6 %copy.21 = bf16[1,8,512]{2,1,0:T(8,128)(2,1)} copy(bf16[1,8,512]{2,1,0:T(8,128)(2,1)S(1)} %get-tuple-element.6) | data formatting | bytes 16384
  29.0 0.6 %copy.22 = f32[1,8,512]{2,1,0:T(8,128)} copy(f32[1,8,512]{2,1,0:T(8,128)S(1)} %get-tuple-element.7) | data formatting | bytes 32768
  29.6 0.6 %copy.23 = f32[1,8,512]{2,1,0:T(8,128)} copy(f32[1,8,512]{2,1,0:T(8,128)S(1)} %get-tuple-element.8) | data formatting | bytes 32768
  (6 shorter events, 0.0 us)
Async XLA Ops:
  0.6 0.7 %copy-start.10 = (s32[1,256]{1,0:T(1,128)S(1)}, s32[1,256]{1,0:T(1,128)}, u32[]{:S(2)}) copy-start(s32[1,256]{1,0:T(1,128)} %tin_ref.1) | copy-start | bytes 3076
  1.3 1.0 %copy-start = (bf16[1,512,512]{2,1,0:T(8,128)(2,1)S(1)}, bf16[1,512,512]{2,1,0:T(8,128)(2,1)}, u32[]{:S(2)}) copy-start(bf16[1,512,512]{2,1,0:T(8,128)(2,1)} %edge_hbm.1) | copy-start | bytes 1572868
  2.4 1.0 %copy-start.1 = (bf16[512,512]{1,0:T(8,128)(2,1)S(1)}, bf16[512,512]{1,0:T(8,128)(2,1)}, u32[]{:S(2)}) copy-start(bf16[512,512]{1,0:T(8,128)(2,1)} %wsrc_hbm.1) | copy-start | bytes 1572868
  3.4 1.0 %copy-start.2 = (bf16[512,512]{1,0:T(8,128)(2,1)S(1)}, bf16[512,512]{1,0:T(8,128)(2,1)}, u32[]{:S(2)}) copy-start(bf16[512,512]{1,0:T(8,128)(2,1)} %wtgt_hbm.1) | copy-start | bytes 1572868
  4.4 1.0 %copy-start.3 = (bf16[512,512]{1,0:T(8,128)(2,1)S(1)}, bf16[512,512]{1,0:T(8,128)(2,1)}, u32[]{:S(2)}) copy-start(bf16[512,512]{1,0:T(8,128)(2,1)} %win_hbm.1) | copy-start | bytes 1572868
  5.5 1.0 %copy-start.4 = (bf16[512,512]{1,0:T(8,128)(2,1)S(1)}, bf16[512,512]{1,0:T(8,128)(2,1)}, u32[]{:S(2)}) copy-start(bf16[512,512]{1,0:T(8,128)(2,1)} %wout_hbm.1) | copy-start | bytes 1572868
  6.5 0.7 %copy-start.5 = (bf16[1,8,512]{2,1,0:T(8,128)(2,1)S(1)}, bf16[1,8,512]{2,1,0:T(8,128)(2,1)}, u32[]{:S(2)}) copy-start(bf16[1,8,512]{2,1,0:T(8,128)(2,1)} %state_ref.1) | copy-start | bytes 24580
  7.2 0.7 %copy-start.6 = (bf16[1,8,512]{2,1,0:T(8,128)(2,1)S(1)}, bf16[1,8,512]{2,1,0:T(8,128)(2,1)}, u32[]{:S(2)}) copy-start(bf16[1,8,512]{2,1,0:T(8,128)(2,1)} %dir_ref.1) | copy-start | bytes 24580
  7.9 0.7 %copy-start.7 = (bf16[1,8,512]{2,1,0:T(8,128)(2,1)S(1)}, bf16[1,8,512]{2,1,0:T(8,128)(2,1)}, u32[]{:S(2)}) copy-start(bf16[1,8,512]{2,1,0:T(8,128)(2,1)} %up_ref.1) | copy-start | bytes 24580
  8.6 0.7 %copy-start.8 = (s32[1,512]{1,0:T(1,128)S(1)}, s32[1,512]{1,0:T(1,128)}, u32[]{:S(2)}) copy-start(s32[1,512]{1,0:T(1,128)} %src_ref.1) | copy-start | bytes 6148
  9.3 0.7 %copy-start.9 = (s32[1,512]{1,0:T(1,128)S(1)}, s32[1,512]{1,0:T(1,128)}, u32[]{:S(2)}) copy-start(s32[1,512]{1,0:T(1,128)} %tgt_ref.1) | copy-start | bytes 6148
  10.0 0.7 %copy-start.11 = (s32[1,256]{1,0:T(1,128)S(1)}, s32[1,256]{1,0:T(1,128)}, u32[]{:S(2)}) copy-start(s32[1,256]{1,0:T(1,128)} %tout_ref.1) | copy-start | bytes 3076
  10.7 0.7 %copy-start.12 = (bf16[1,256]{1,0:T(2,128)(2,1)S(1)}, bf16[1,256]{1,0:T(2,128)(2,1)}, u32[]{:S(2)}) copy-start(bf16[1,256]{1,0:T(2,128)(2,1)} %coef_ref.1) | copy-start | bytes 1540

commit v2 on v1

--- a/solution.py
+++ b/solution.py
@@ -35,8 +35,39 @@
     return x[:half] + x[half:]
 
 
+def peers_of(me, n):
+    if n & (n - 1):
+        return [lax.rem(me + k, n) for k in range(1, n)]
+    peers = []
+    for j in range(n - 1, 0, -1):
+        peer, bit = me, 1
+        while bit < n:
+            if j & bit:
+                peer = peer + bit * (1 - 2 * lax.rem(me // bit, 2))
+            bit *= 2
+        peers.append(peer)
+    return peers
+
+
 def kernel(
     n,
+    state_hbm,
+    dir_hbm,
+    up_hbm,
+    src_hbm,
+    tgt_hbm,
+    blocks_hbm,
+    tin_hbm,
+    tout_hbm,
+    coef_hbm,
+    edge_hbm,
+    wsrc_hbm,
+    wtgt_hbm,
+    win_hbm,
+    wout_hbm,
+    upd_hbm,
+    grad_hbm,
+    hvp_hbm,
     state_ref,
     dir_ref,
     up_ref,
@@ -46,14 +77,6 @@
     tin_ref,
     tout_ref,
     coef_ref,
-    edge_hbm,
-    wsrc_hbm,
-    wtgt_hbm,
-    win_hbm,
-    wout_hbm,
-    upd_out,
-    grad_out,
-    hvp_out,
     edge_v,
     wsrc_v,
     wtgt_v,
@@ -78,6 +101,10 @@
     c_recv,
     p_send,
     p_recv,
+    upd_v,
+    grad_v,
+    hvp_v,
+    store_sem,
 ):
     me = lax.axis_index("graph")
     other = 1 - lax.axis_index("feat")
@@ -88,9 +115,24 @@
     trips = tin_ref.shape[1]
     half = width // 2
 
+    peers = peers_of(me, n)
+    barrier = pltpu.get_barrier_semaphore()
+    for peer in peers:
+        pl.semaphore_signal(barrier, inc=1, device_id={"graph": peer}, device_id_type=MESH)
+    pl.semaphore_signal(barrier, inc=1, device_id={"feat": other}, device_id_type=MESH)
+
     loads = []
     for i, (s, d) in enumerate(
         (
+            (state_hbm, state_ref),
+            (dir_hbm, dir_ref),
+            (up_hbm, up_ref),
+            (src_hbm, src_ref),
+            (tgt_hbm, tgt_ref),
+            (tin_hbm, tin_ref),
+            (tout_hbm, tout_ref),
+            (coef_hbm, coef_ref),
+            (blocks_hbm, blocks_ref),
             (edge_hbm.at[0], edge_v),
             (win_hbm, win_v),
             (wout_hbm, wout_v),
@@ -102,13 +144,8 @@
         c.start()
         loads.append(c)
 
-    barrier = pltpu.get_barrier_semaphore()
-    for k in range(1, n):
-        pl.semaphore_signal(
-            barrier, inc=1, device_id={"graph": lax.rem(me + k, n)}, device_id_type=MESH
-        )
-    pl.semaphore_signal(barrier, inc=1, device_id={"feat": other}, device_id_type=MESH)
-
+    for c in loads[:3]:
+        c.wait()
     up = up_ref[0].astype(F32)
     mine = jnp.concatenate(
         [
@@ -122,18 +159,20 @@
     pl.semaphore_wait(barrier, n)
 
     gathers = []
-    for k in range(1, n):
+    for k, peer in enumerate(peers):
         c = pltpu.make_async_remote_copy(
             src_ref=stage,
             dst_ref=gathered.at[me],
-            send_sem=g_send.at[k - 1],
-            recv_sem=g_recv.at[k - 1],
-            device_id={"graph": lax.rem(me + k, n)},
+            send_sem=g_send.at[k],
+            recv_sem=g_recv.at[k],
+            device_id={"graph": peer},
             device_id_type=MESH,
         )
         c.start()
         gathers.append(c)
 
+    for c in loads[3:9]:
+        c.wait()
     src_col = as_column(src_ref[...])
     tgt_row = tgt_ref[...]
     tgt_col = as_column(tgt_row)
@@ -168,13 +207,15 @@
     spread_t = jnp.transpose(spread_split[:, : 2 * pair]).astype(BF16)
     spread_split = spread_split.astype(BF16)
 
-    loads[0].wait()
+    loads[9].wait()
     picked = mm(in_hot, edge_v[...]).astype(BF16)
     mixed = edge_v[...].astype(F32) + mm(out_weighted, picked)
-    loads[1].wait()
+    loads[10].wait()
     hidden_edge = mm(mixed.astype(BF16), win_v[...])
-    for c in loads[2:]:
+    for c in loads[11:]:
         c.wait()
+    src_in = mm(wsrc_v[...], win_v[...]).astype(BF16)
+    tgt_in = mm(wtgt_v[...], win_v[...]).astype(BF16)
 
     for c in gathers:
         c.wait_recv()
@@ -189,18 +230,12 @@
         axis=1,
     ).astype(BF16)
     both = jnp.concatenate([state, direction], axis=0).astype(BF16)
-    proj_src = mm(both, wsrc_v[...])
-    proj_tgt = mm(both, wtgt_v[...])
-    proj = jnp.concatenate(
-        [
-            proj_src[:all_atoms],
-            proj_tgt[:all_atoms],
-            proj_src[all_atoms:],
-            proj_tgt[all_atoms:],
-        ],
+    via_src = mm(both, src_in)
+    via_tgt = mm(both, tgt_in)
+    proj_hidden = jnp.concatenate(
+        [via_src[:all_atoms], via_tgt[:all_atoms], via_src[all_atoms:], via_tgt[all_atoms:]],
         axis=0,
-    ).astype(BF16)
-    proj_hidden = mm(proj, win_v[...])
+    )
     high = proj_hidden.astype(BF16)
     low = (proj_hidden - high.astype(F32)).astype(BF16)
     hidden_pre = hidden_edge + mm(
@@ -226,13 +261,12 @@
         upd_own[p] = packed
         upd_send[p] = packed.astype(BF16)
     updates = []
-    for k in range(1, n):
-        peer = lax.rem(me + k, n)
+    for k, peer in enumerate(peers):
         c = pltpu.make_async_remote_copy(
             src_ref=upd_send.at[peer],
-            dst_ref=upd_recv.at[k - 1],
-            send_sem=u_send.at[k - 1],
-            recv_sem=u_recv.at[k - 1],
+            dst_ref=upd_recv.at[k],
+            send_sem=u_send.at[k],
+            recv_sem=u_recv.at[k],
             device_id={"graph": peer},
             device_id_type=MESH,
         )
@@ -242,12 +276,9 @@
     via = jnp.concatenate(
         [join_rows(mm(spread_t, hid_cot)), join_rows(mm(spread_t, tan_hid_cot))], axis=0
     )
-    via = join_rows(mm_nt(split_rows(via), win_v[...]))
     via_src = jnp.concatenate([via[:all_atoms], via[pair : pair + all_atoms]], axis=0)
     via_tgt = jnp.concatenate([via[all_atoms:pair], via[pair + all_atoms :]], axis=0)
-    grads = join_rows(
-        mm_nt(split_rows(via_src), wsrc_v[...]) + mm_nt(split_rows(via_tgt), wtgt_v[...])
-    )
+    grads = join_rows(mm_nt(split_rows(via_src), src_in) + mm_nt(split_rows(via_tgt), tgt_in))
     for p in range(n):
         packed = jnp.concatenate(
             [
@@ -259,13 +290,12 @@
         cot_own[p] = packed
         cot_send[p] = packed.astype(BF16)
     cots = []
-    for k in range(1, n):
-        peer = lax.rem(me + k, n)
+    for k, peer in enumerate(peers):
         c = pltpu.make_async_remote_copy(
             src_ref=cot_send.at[peer],
-            dst_ref=cot_recv.at[k - 1],
-            send_sem=c_send.at[k - 1],
-            recv_sem=c_recv.at[k - 1],
+            dst_ref=cot_recv.at[k],
+            send_sem=c_send.at[k],
+            recv_sem=c_recv.at[k],
             device_id={"graph": peer},
             device_id_type=MESH,
         )
@@ -273,13 +303,13 @@
         cots.append(c)
 
     upd_sum = upd_own[me]
-    for k in range(1, n):
-        updates[k - 1].wait_recv()
-        upd_sum = upd_sum + upd_recv[k - 1].astype(F32)
+    for k in range(n - 1):
+        updates[k].wait_recv()
+        upd_sum = upd_sum + upd_recv[k].astype(F32)
     cot_sum = cot_own[me]
-    for k in range(1, n):
-        cots[k - 1].wait_recv()
-        cot_sum = cot_sum + cot_recv[k - 1].astype(F32)
+    for k in range(n - 1):
+        cots[k].wait_recv()
+        cot_sum = cot_sum + cot_recv[k].astype(F32)
     total = jnp.concatenate([cot_sum, upd_sum], axis=1)
     pair_send[...] = total
     c = pltpu.make_async_remote_copy(
@@ -293,14 +323,26 @@
     c.start()
     c.wait_recv()
     total = total + pair_recv[...]
-    grad_out[0] = total[:atoms, :width]
-    hvp_out[0] = total[atoms:, :width]
-    upd_out[0] = jnp.concatenate([total[:atoms, width:], total[atoms:, width:]], axis=1).astype(
-        BF16
-    )
+    upd_v[0] = jnp.concatenate([total[:atoms, width:], total[atoms:, width:]], axis=1).astype(BF16)
+    grad_v[0] = total[:atoms, :width]
+    hvp_v[0] = total[atoms:, :width]
+    stores = [
+        pltpu.make_async_copy(v, hbm, store_sem.at[i])
+        for i, (v, hbm) in enumerate(((upd_v, upd_hbm), (grad_v, grad_hbm), (hvp_v, hvp_hbm)))
+    ]
+    for s in stores:
+        s.start()
     c.wait_send()
     for c in gathers + updates + cots:
         c.wait_send()
+    for s in stores:
+        s.wait()
+
+
+def write_out(upd_ref, grad_ref, hvp_ref, upd_out, grad_out, hvp_out):
+    upd_out[...] = upd_ref[...]
+    grad_out[...] = grad_ref[...]
+    hvp_out[...] = hvp_ref[...]
 
 
 def on_device(
@@ -324,21 +366,30 @@
     slots = edge_state.shape[1]
     hidden = w_in.shape[1]
     half = width // 2
-    vmem = pl.BlockSpec(memory_space=pltpu.VMEM)
-    smem = pl.BlockSpec(memory_space=pltpu.SMEM)
-    far = pl.BlockSpec(memory_space=pl.ANY)
+    trips = trip_in.shape[1]
+    far = pl.BlockSpec(memory_space=pltpu.HBM)
     dma = pltpu.SemaphoreType.DMA
-    return pl.pallas_call(
+    outs = (
+        jax.ShapeDtypeStruct((1, atoms, width), BF16),
+        jax.ShapeDtypeStruct((1, atoms, width), F32),
+        jax.ShapeDtypeStruct((1, atoms, width), F32),
+    )
+    results = pl.pallas_call(
         functools.partial(kernel, n),
         name="interaction",
-        out_shape=(
-            jax.ShapeDtypeStruct((1, atoms, width), BF16),
-            jax.ShapeDtypeStruct((1, atoms, width), F32),
-            jax.ShapeDtypeStruct((1, atoms, width), F32),
-        ),
-        in_specs=[vmem] * 5 + [smem] + [vmem] * 3 + [far] * 5,
-        out_specs=(vmem, vmem, vmem),
+        out_shape=outs,
+        in_specs=[far] * 14,
+        out_specs=(far, far, far),
         scratch_shapes=[
+            pltpu.VMEM((1, atoms, width), BF16),
+            pltpu.VMEM((1, atoms, width), BF16),
+            pltpu.VMEM((1, atoms, width), BF16),
+            pltpu.VMEM((1, slots), jnp.int32),
+            pltpu.VMEM((1, slots), jnp.int32),
+            pltpu.SMEM((1, 1), jnp.int32),
+            pltpu.VMEM((1, trips), jnp.int32),
+            pltpu.VMEM((1, trips), jnp.int32),
+            pltpu.VMEM((1, trips), BF16),
             pltpu.VMEM((slots, width), BF16),
             pltpu.VMEM((width, width), BF16),
             pltpu.VMEM((width, width), BF16),
@@ -354,7 +405,7 @@
             pltpu.VMEM((n - 1, 2 * atoms, width), BF16),
             pltpu.VMEM((2 * atoms, width + half), F32),
             pltpu.VMEM((2 * atoms, width + half), F32),
-            dma((5,)),
+            dma((14,)),
             dma((n - 1,)),
             dma((n - 1,)),
             dma((n - 1,)),
@@ -363,9 +414,11 @@
             dma((n - 1,)),
             dma,
             dma,
-        ],
+        ]
+        + [pltpu.VMEM(o.shape, o.dtype) for o in outs]
+        + [dma((3,))],
         compiler_params=pltpu.CompilerParams(
-            collective_id=0, has_side_effects=True, vmem_limit_bytes=48 * 1024 * 1024
+            collective_id=0, has_side_effects=True, vmem_limit_bytes=64 * 1024 * 1024
         ),
     )(
         atom_state,
@@ -383,6 +436,12 @@
         w_in,
         w_out,
     )
+    return pl.pallas_call(
+        write_out,
+        name="write_out",
+        out_shape=outs,
+        compiler_params=pltpu.CompilerParams(vmem_limit_bytes=64 * 1024 * 1024),
+    )(*results)
 
 
 def solution(mesh):

time: 30.8 us -> 19.6 us (0.64)
  the two profiles are of different devices: /device:TPU:0 before, /device:TPU:1 now
where the time goes in v2:
time: 19.6 us; the launch traced here: 19.3 us
  Pallas kernels  18 us (92%)
  between operations  1.29 us (7%)
    pallas_call x1, Pallas kernels, on_device(): pl.pallas_call(functools.partial(kernel, n), name='interaction', out_shap...  16.6 us
    pallas_call x1, Pallas kernels, on_device(): pl.pallas_call(write_out, name='write_out', out_shape=outs, compiler_para...  1.37 us

profile of v2, /device:TPU:1, one launch (start us, length us, event | category | flops | bytes accessed | tf_op | source)
XLA Modules:
  0.0 19.3 jit_solution(14024070446444633401)
XLA Ops:
  1.3 16.6 %interaction.1 = (bf16[1,8,512]{2,1,0:T(8,128)(2,1)}, f32[1,8,512]{2,1,0:T(8,128)}, f32[1,8,512]{2,1,0:T(8,128)}) custom-call(bf16[1,8,512]{2,1,0:T(8,128)(2,1)} %state_hbm.1, bf16[1,8,512]{2,1,0:T(8,128)(2,1)} %dir_hbm.1, bf16[1,8,512]{2,1,0:T(8,128)(2,1)} %up_hbm.1, s32[1,512]{1,0:T(1,128)} %src_hbm.1, s32[1,512]{1,0:T(1,128)} %tgt_hbm.1, ...), custom_call_target="tpu_custom_call" | custom-call | tf_op jit(solution)/shard_map/interaction/pallas_call | solution.py:377
  17.9 1.4 %write_out.1 = (bf16[1,8,512]{2,1,0:T(8,128)(2,1)}, f32[1,8,512]{2,1,0:T(8,128)}, f32[1,8,512]{2,1,0:T(8,128)}) custom-call(bf16[1,8,512]{2,1,0:T(8,128)(2,1)} %get-tuple-element.6.upd_ref, f32[1,8,512]{2,1,0:T(8,128)} %get-tuple-element.7.grad_ref, f32[1,8,512]{2,1,0:T(8,128)} %get-tuple-element.8.hvp_ref), custom_call_target="tpu_custom_call" | custom-call | tf_op jit(solution)/shard_map/write_out/pallas_call | solution.py:439

commit v3 on v2

--- a/solution.py
+++ b/solution.py
@@ -156,21 +156,6 @@
     ).astype(BF16)
     stage[...] = mine
     gathered[me] = mine
-    pl.semaphore_wait(barrier, n)
-
-    gathers = []
-    for k, peer in enumerate(peers):
-        c = pltpu.make_async_remote_copy(
-            src_ref=stage,
-            dst_ref=gathered.at[me],
-            send_sem=g_send.at[k],
-            recv_sem=g_recv.at[k],
-            device_id={"graph": peer},
-            device_id_type=MESH,
-        )
-        c.start()
-        gathers.append(c)
-
     for c in loads[3:9]:
         c.wait()
     src_col = as_column(src_ref[...])
@@ -207,6 +192,21 @@
     spread_t = jnp.transpose(spread_split[:, : 2 * pair]).astype(BF16)
     spread_split = spread_split.astype(BF16)
 
+    pl.semaphore_wait(barrier, n)
+
+    gathers = []
+    for k, peer in enumerate(peers):
+        c = pltpu.make_async_remote_copy(
+            src_ref=stage,
+            dst_ref=gathered.at[me],
+            send_sem=g_send.at[k],
+            recv_sem=g_recv.at[k],
+            device_id={"graph": peer},
+            device_id_type=MESH,
+        )
+        c.start()
+        gathers.append(c)
+
     loads[9].wait()
     picked = mm(in_hot, edge_v[...]).astype(BF16)
     mixed = edge_v[...].astype(F32) + mm(out_weighted, picked)
@@ -246,11 +246,12 @@
     )
     act_cot = mm(tgt_hot, split_rows(mm_nt(upstream, wout_v[...])))
 
-    sig = jax.nn.sigmoid(hidden_pre)
+    tanh = jnp.tanh(0.5 * hidden_pre)
+    sig = 0.5 + 0.5 * tanh
+    bell = 0.25 - 0.25 * (tanh * tanh)
     activation = (hidden_pre * sig).astype(BF16)
-    rest = 1.0 - sig
-    first_slope = sig * (1.0 + hidden_pre * rest)
-    second_slope = sig * rest * (2.0 + hidden_pre * (1.0 - 2.0 * sig))
+    first_slope = sig + hidden_pre * bell
+    second_slope = bell * (2.0 - hidden_pre * tanh)
     hid_cot = (act_cot * first_slope).astype(BF16)
     tan_hid_cot = (act_cot * second_slope * tan_hidden).astype(BF16)
 

time: 19.6 us -> 19.5 us (level)
  no operation moved by 1% of the time
where the time goes in v3:
time: 19.5 us; the launch traced here: 19.2 us
  Pallas kernels  17.9 us (92%)
  between operations  1.29 us (7%)
    pallas_call x1, Pallas kernels, on_device(): pl.pallas_call(functools.partial(kernel, n), name='interaction', out_shap...  16.5 us
    pallas_call x1, Pallas kernels, on_device(): pl.pallas_call(write_out, name='write_out', out_shape=outs, compiler_para...  1.37 us

profile of v3, /device:TPU:1, one launch (start us, length us, event | category | flops | bytes accessed | tf_op | source)
XLA Modules:
  0.0 19.2 jit_solution(3464141078633088950)
XLA Ops:
  1.3 16.5 %interaction.1 = (bf16[1,8,512]{2,1,0:T(8,128)(2,1)}, f32[1,8,512]{2,1,0:T(8,128)}, f32[1,8,512]{2,1,0:T(8,128)}) custom-call(bf16[1,8,512]{2,1,0:T(8,128)(2,1)} %state_hbm.1, bf16[1,8,512]{2,1,0:T(8,128)(2,1)} %dir_hbm.1, bf16[1,8,512]{2,1,0:T(8,128)(2,1)} %up_hbm.1, s32[1,512]{1,0:T(1,128)} %src_hbm.1, s32[1,512]{1,0:T(1,128)} %tgt_hbm.1, ...), custom_call_target="tpu_custom_call" | custom-call | tf_op jit(solution)/shard_map/interaction/pallas_call | solution.py:378
  17.8 1.4 %write_out.1 = (bf16[1,8,512]{2,1,0:T(8,128)(2,1)}, f32[1,8,512]{2,1,0:T(8,128)}, f32[1,8,512]{2,1,0:T(8,128)}) custom-call(bf16[1,8,512]{2,1,0:T(8,128)(2,1)} %get-tuple-element.6.upd_ref, f32[1,8,512]{2,1,0:T(8,128)} %get-tuple-element.7.grad_ref, f32[1,8,512]{2,1,0:T(8,128)} %get-tuple-element.8.hvp_ref), custom_call_target="tpu_custom_call" | custom-call | tf_op jit(solution)/shard_map/write_out/pallas_call | solution.py:440
